TPU v7x, 32 devices: a whole 2x2x4 slice. The times are simulated.
32 devices in a mesh: depth: 4 (over y, core), lat: 8 (over z, x).
Axes of the slice: x: 2, y: 2, z: 4, core: 2. Of those that a mesh axis runs over, the one named last changes fastest.
Arguments:
- slices: float32 [12, 2, 256, 2048], P('depth', None, None, 'lat'), may hold values from -1.23 to 1.23, as said below
- section_counts: int32 [4], P('depth'), may hold values from 1 to 3, as said below
- scan_rows: int32 [64], P('lat'), may hold values from 0 to 128, as said below
- scan_columns: int32 [64], P('lat'), may hold values from 0 to 256, as said below
- tick_order: int32 [8, 8], P('lat'), may hold values from 0 to 7, each once within a row
- measured: float32 [64, 128, 128], P('lat'), may hold values from 0.2 to 2
- illumination: float32 [2, 128, 128], replicated, may hold values from -4.2 to 4.2
Outputs:
- slice_grad: float32 [12, 2, 256, 2048], P('depth', None, None, 'lat')
- position_loss: float32 [8, 8], P('lat')
Inputs may be any that keep to these rules, and one draw needn't show every extreme that they name: `slices`: the real and imaginary parts of transmission values of magnitude near one. `section_counts`: some section uses all 3 slots and some other section uses one. `scan_rows`: both ends are reached in every draw. `scan_columns`: a window may reach up to 128 columns into the next tile, the last tile continuing into the first; both ends are reached in every draw. `tick_order`: each row lists the tile's 8 positions once.
All inputs are finite; a program needn't handle non-finite values.
Results may differ from a plain program's by a relative error of at most 0.0003.
Values sent between devices are 32-bit elements; how exact they have to be, the bound alone decides.
A program may use at most 128 MiB of HBM per device.

v0:
```python
import functools
import math

import jax
import jax.numpy as jnp
import ml_dtypes
import numpy as np
from jax import lax
from jax.experimental import pallas as pl
from jax.experimental.pallas import tpu as pltpu
from jax.sharding import PartitionSpec as P

fresnel = 12.0


def split_table(matrix):
    coarse = matrix.astype(ml_dtypes.bfloat16)
    fine = (matrix - coarse.astype(np.float64)).astype(ml_dtypes.bfloat16)
    return np.stack([coarse, fine])


def make_tables(width):
    index = np.arange(width)
    angle = 2.0 * math.pi / width * (index[:, None] * index[None, :] % width)
    dft = np.exp(-1j * angle) / math.sqrt(width)
    frequency = ((index + width // 2) % width - width // 2) / width
    spread = np.conj(dft) @ (np.exp(-1j * fresnel * frequency**2)[:, None] * dft)
    tables = []
    for matrix in (spread, dft):
        right = np.block([[matrix.real, matrix.imag], [-matrix.imag, matrix.real]])
        left = np.block([[matrix.real, -matrix.imag], [matrix.imag, matrix.real]])
        tables.append(np.stack([split_table(right), split_table(left)]))
    return np.stack(tables)


def halves(value):
    coarse = value.astype(jnp.bfloat16)
    fine = (value - coarse.astype(jnp.float32)).astype(jnp.bfloat16)
    return coarse, fine


def both_sides(parts, tables, which, adjoint):
    width = parts[0].shape[0]
    first, second = (1, 0) if adjoint else (0, 1)
    coarse, fine = halves(jnp.concatenate(parts, axis=0))
    high, low = tables[which, first, 0], tables[which, first, 1]
    half = jnp.dot(
        jnp.concatenate([coarse, fine, coarse], axis=1),
        jnp.concatenate([high, high, low], axis=0),
        preferred_element_type=jnp.float32,
    )
    rows = [half[p * width : (p + 1) * width] for p in range(len(parts))]
    turned = jnp.concatenate(
        [
            jnp.concatenate([r[:, :width] for r in rows], axis=1),
            jnp.concatenate([r[:, width:] for r in rows], axis=1),
        ],
        axis=0,
    )
    coarse, fine = halves(turned)
    high, low = tables[which, second, 0], tables[which, second, 1]
    full = jnp.dot(
        jnp.concatenate([high, high, low], axis=1),
        jnp.concatenate([coarse, fine, coarse], axis=0),
        preferred_element_type=jnp.float32,
    )
    return [
        (full[:width, p * width : (p + 1) * width], full[width:, p * width : (p + 1) * width])
        for p in range(len(parts))
    ]


def stage_kernel(kind, stage, cfg, *refs):
    group, slots, width, tile, share = cfg
    blocks = tile // width
    refs = list(refs)
    meta, tables_hbm, entering_hbm = refs[:3]
    mains, rims = refs[3 : 3 + group], refs[3 + group : 3 + 2 * group]
    refs = refs[3 + 2 * group :]
    if kind == "T":
        measured_hbm, out_hbm, loss_ref = refs[0], refs[1], refs[2 + 2 * group]
        grads = refs[2 : 2 + 2 * group]
        refs = refs[3 + 2 * group :]
    elif kind == "F":
        out_hbm, inner_hbm = refs[0], refs[1]
        refs = refs[2:]
    else:
        inner_hbm = refs[0]
        out_hbm = refs[1 + 2 * group]
        grads = refs[2 + 2 * group : 2 + 4 * group]
        refs = refs[2 + 4 * group :]
    specimen, store, inner, current, tables, wanted, sems = refs

    @pl.when(meta[0] == stage)
    def _():
        core = meta[1]
        copies = []

        def bring(source, target):
            copy = pltpu.make_async_copy(source, target, sems.at[len(copies)])
            copy.start()
            copies.append(copy)

        bring(tables_hbm, tables)
        for j in range(group):
            section = core if j == 0 else 1 - core
            place = pl.ds(section * slots, slots)
            for b in range(blocks):
                bring(mains[j].at[:, :, :, pl.ds(b * width, width)], specimen.at[place, :, b])
            bring(rims[j], specimen.at[place, :, blocks])
        if kind == "B":
            bring(entering_hbm, current)
            bring(inner_hbm, inner)
        else:
            bring(entering_hbm, inner.at[0])
        if kind == "T":
            bring(measured_hbm.at[pl.ds(core * share, share)], wanted)
        if kind != "F":
            for slot in range(group * slots):
                store[slot] = jnp.zeros(store.shape[1:], jnp.float32)
        for copy in copies:
            copy.wait()

        count = meta[2]
        total = meta[2] + meta[3] if group == 2 else meta[2]
        lane = lax.broadcasted_iota(jnp.int32, (width, width), 1)

        def place_of(step):
            later = step >= count
            return jnp.where(later, slots + step - count, step)

        def corner(p):
            row, column = meta[4 + p], meta[4 + share + p]
            block = jnp.minimum(column // width, blocks - 1)
            return row, block, column - block * width

        def window(slot, p):
            row, block, shift = corner(p)
            back = lax.rem(width - shift, width)
            found = []
            for c in range(2):
                here = specimen[slot, c, block, pl.ds(row, width), :]
                after = specimen[slot, c, block + 1, pl.ds(row, width), :]
                found.append(pltpu.roll(jnp.where(lane >= shift, here, after), back, 1))
            return found

        def deposit(slot, p, pull):
            row, block, shift = corner(p)
            turn = lax.rem(shift, width)
            for c in range(2):
                turned = pltpu.roll(pull[c], turn, 1)
                here = jnp.where(lane >= shift, turned, 0.0)
                store[slot, c, block, pl.ds(row, width), :] += here
                store[slot, c, block + 1, pl.ds(row, width), :] += turned - here

        def which(step):
            return jnp.where(step == total - 1, 1, 0) if kind == "T" else 0

        def forward(step, carry):
            slot = place_of(step)
            parts = []
            for p in range(share):
                real, imag = window(slot, p)
                value = inner[step, p]
                first, second = value[:, :width], value[:, width:]
                parts.append(
                    jnp.concatenate(
                        [first * real - second * imag, first * imag + second * real], axis=1
                    )
                )
            results = both_sides(parts, tables, which(step), False)
            for p in range(share):
                inner[step + 1, p] = jnp.concatenate(results[p], axis=1)
            return carry

        def backward(back_step, carry):
            step = total - 1 - back_step
            slot = place_of(step)
            parts = [current[p] for p in range(share)]
            results = both_sides(parts, tables, which(step), True)
            for p in range(share):
                first, second = results[p]
                value = inner[step, p]
                real, imag = value[:, :width], value[:, width:]
                deposit(
                    slot, p, (real * first + imag * second, real * second - imag * first)
                )
                real, imag = window(slot, p)
                current[p] = jnp.concatenate(
                    [real * first + imag * second, real * second - imag * first], axis=1
                )
            return carry

        if kind != "B":
            lax.fori_loop(0, total, forward, 0)
        if kind == "T":
            for p in range(share):
                value = inner[total, p]
                first, second = value[:, :width], value[:, width:]
                misfit = first * first + second * second - wanted[p]
                loss = jnp.sum(misfit * misfit) / (width * width)
                loss_ref[p : p + 1, :] = jnp.full((1, 128), loss, jnp.float32)
                factor = 4.0 * misfit
                current[p] = jnp.concatenate([factor * first, factor * second], axis=1)
        if kind != "F":
            lax.fori_loop(0, total, backward, 0)

        copies.clear()
        if kind == "F":
            bring(inner.at[total], out_hbm)
            bring(inner, inner_hbm)
        else:
            bring(current, out_hbm)
            for j in range(group):
                section = core if j == 0 else 1 - core
                place = pl.ds(section * slots, slots)
                for b in range(blocks):
                    bring(store.at[place, :, b], grads[j].at[:, :, :, pl.ds(b * width, width)])
                bring(store.at[place, :, blocks], grads[group + j])
        for copy in copies:
            copy.wait()


def stage_call(kind, stage, cfg, operands, kept=()):
    group, slots, width, tile, share = cfg
    blocks = tile // width
    f32 = jnp.float32
    field = jax.ShapeDtypeStruct((share, width, 2 * width), f32)
    inner_shape = (group * slots + 1, share, width, 2 * width)
    grads = [jax.ShapeDtypeStruct((slots, 2, tile, tile), f32)] * group
    grads += [jax.ShapeDtypeStruct((slots, 2, tile, width), f32)] * group
    anywhere = pl.BlockSpec(memory_space=pl.ANY)
    scalars = pl.BlockSpec(memory_space=pltpu.SMEM)
    if kind == "F":
        outs = [field, jax.ShapeDtypeStruct(inner_shape, f32)]
    else:
        outs = [field] + grads
    out_specs = [anywhere] * len(outs)
    if kind == "T":
        outs.append(jax.ShapeDtypeStruct((share, 128), f32))
        out_specs.append(pl.BlockSpec(memory_space=pltpu.VMEM))
    aliases = {}
    for i in range(len(kept)):
        aliases[len(operands) + i] = 1 + i
    operands = list(operands) + list(kept)
    body = functools.partial(stage_kernel, kind, stage, cfg)
    if kind == "F" and kept:
        at = len(operands) - 1

        def body(*refs):
            stage_kernel(kind, stage, cfg, *refs[:at], *refs[at + 1 :])

    return pl.pallas_call(
        body,
        out_shape=outs,
        in_specs=[scalars] + [anywhere] * (len(operands) - 1),
        out_specs=out_specs,
        input_output_aliases=aliases,
        scratch_shapes=[
            pltpu.VMEM((group * slots, 2, blocks + 1, tile, width), f32),
            pltpu.VMEM((group * slots, 2, blocks + 1, tile, width), f32),
            pltpu.VMEM(inner_shape, f32),
            pltpu.VMEM((share, width, 2 * width), f32),
            pltpu.VMEM((2, 2, 2, 2 * width, 2 * width), jnp.bfloat16),
            pltpu.VMEM((share, width, width), f32),
            pltpu.SemaphoreType.DMA((8 + group * (blocks + 1),)),
        ],
        compiler_params=pltpu.CompilerParams(vmem_limit_bytes=48 * 1024 * 1024),
        name="stage_" + kind,
    )(*operands)


def shards(slices, section_counts, scan_rows, scan_columns, tick_order, measured, illumination):
    width = illumination.shape[-1]
    slots, _, tile, _ = slices.shape
    positions = scan_rows.shape[0]
    depth = lax.axis_size("depth")
    lat = lax.axis_size("lat")
    group = 2 if depth % 2 == 0 and positions % 2 == 0 else 1
    stages = depth // group
    share = positions // group
    cfg = (group, slots, width, tile, share)
    segment = lax.axis_index("depth")
    core = lax.rem(segment, group)
    stage = lax.div(segment, group)
    swap = [(d, d + 1 - 2 * (d % 2)) for d in range(depth)]

    def partner(block):
        return lax.ppermute(block, "depth", swap)

    def move(block, source, target):
        route = [(source * group + c, target * group + c) for c in range(group)]
        return lax.ppermute(block, "depth", route)

    rim = lax.ppermute(slices[..., :width], "lat", [((i + 1) % lat, i) for i in range(lat)])
    if group == 2:
        mains, rims = [slices, partner(slices)], [rim, partner(rim)]
        other = partner(section_counts)
        counts = jnp.where(
            core == 0,
            jnp.concatenate([section_counts, other]),
            jnp.concatenate([other, section_counts]),
        )
    else:
        mains, rims = [slices], [rim]
        counts = jnp.concatenate([section_counts, jnp.zeros_like(section_counts)])
    meta = jnp.concatenate(
        [
            jnp.stack([stage, core]),
            counts,
            lax.dynamic_slice_in_dim(scan_rows, core * share, share, 0),
            lax.dynamic_slice_in_dim(scan_columns, core * share, share, 0),
        ]
    ).astype(jnp.int32)
    tables = jnp.asarray(make_tables(width))
    launch = jnp.concatenate([illumination[0], illumination[1]], axis=1)
    field = jnp.broadcast_to(launch, (share, width, 2 * width))
    shared = (*mains, *rims)
    inner = ()
    for s in range(stages - 1):
        field, kept = stage_call("F", s, cfg, (meta, tables, field, *shared), inner)
        inner = (kept,)
        field = move(field, s, s + 1)
    last = stages - 1
    pull, *grads, loss = stage_call("T", last, cfg, (meta, tables, field, *shared, measured))
    losses = lax.all_gather(loss[:, 0], "depth", axis=0, tiled=True)[last * group * share :]
    for s in range(last - 1, -1, -1):
        pull = move(pull, s + 1, s)
        pull, *grads = stage_call(
            "B", s, cfg, (meta, tables, pull, *shared, inner[0]), tuple(grads)
        )
    main, over = grads[0], grads[group]
    if group == 2:
        over = over + partner(grads[group + 1])
        main = main + partner(grads[1])
    overflow = lax.ppermute(over, "lat", [(i, (i + 1) % lat) for i in range(lat)])
    slice_grad = main.at[..., :width].add(overflow)
    return (slice_grad, losses[tick_order[0]].reshape(1, positions))


def solution(mesh):
    placed = (
        P("depth", None, None, "lat"),
        P("depth"),
        P("lat"),
        P("lat"),
        P("lat", None),
        P("lat", None, None),
        P(),
    )
    return jax.shard_map(
        shards,
        mesh=mesh,
        in_specs=placed,
        out_specs=(P("depth", None, None, "lat"), P("lat", None)),
        check_vma=False,
    )
```

profile of v0, /device:TPU:0, one launch (start us, length us, event | category | flops | bytes accessed | tf_op | source)
XLA Modules:
  0.0 125.3 jit_solution(13337566687265770001)
XLA Ops:
  0.6 0.0 copy-start
  0.6 0.0 copy-start.1
  0.7 1.3 %slice.46 = f32[3,2,256,128]{3,2,1,0:T(8,128)S(1)} slice(f32[3,2,256,256]{3,2,1,0:T(8,128)} %refs_3_.5), slice={[0:3], [0:2], [0:256], [0:128]} | slice | bytes 1572864 | tf_op jit(solution)/shard_map/slice | solution.py:295
  2.0 6.0 %collective-permute-start.2 = (f32[3,2,256,128]{3,2,1,0:T(8,128)S(1)}, f32[3,2,256,128]{3,2,1,0:T(8,128)S(1)}, u32[]{:S(2)}, u32[]{:S(2)}) collective-permute-start(f32[3,2,256,128]{3,2,1,0:T(8,128)S(1)} %slice.46), channel_id=1, source_target_pairs={{1,0},{2,1},{3,2},{4,3},{5,4},{6,5},{7,6},{0,7},{9,8},{10,9},{11,1... | collective-permute-start | bytes 2359304 | tf_op jit(solution)/shard_map/ppermute | solution.py:295
  8.0 0.0 copy-done
  8.0 0.0 collective-permute-start.1
  8.0 16.8 %collective-permute-done.2.refs_5_ = f32[3,2,256,128]{3,2,1,0:T(8,128)S(1)} collective-permute-done((f32[3,2,256,128]{3,2,1,0:T(8,128)S(1)}, f32[3,2,256,128]{3,2,1,0:T(8,128)S(1)}, u32[]{:S(2)}, u32[]{:S(2)}) %collective-permute-start.2) | collective-permute-done | bytes 786464 | tf_op jit(solution)/shard_map/ppermute | solution.py:295
  24.8 0.0 collective-permute-start.3
  24.8 0.5 collective-permute-start
  26.0 0.7 dynamic_slice.6
  26.7 0.7 dynamic_slice.7
  27.5 0.9 slice_bitcast_fusion.1
  28.4 0.0 collective-permute-done
  28.4 0.7 broadcast_select_fusion
  29.1 0.1 concatenate.16.refs_0_
  29.1 0.0 collective-permute-done.3.refs_6_
  29.2 0.0 collective-permute-done.1.refs_4_
  29.2 0.0 copy-done.1
  29.2 0.0 copy-start.2
  29.2 8.8 %stage_F.1 = (f32[4,128,256]{2,1,0:T(8,128)S(1)}, f32[7,4,128,256]{3,2,1,0:T(8,128)}) custom-call(s32[12]{0:T(128)S(1)} %concatenate.16.refs_0_, bf16[2,2,2,256,256]{4,3,2,1,0:T(8,128)(2,1)S(1)} %copy-done.1, f32[4,128,256]{2,1,0:T(8,128)S(1)} %broadcast_in_dim.4.refs_2_, f32[3,2,256,256]{3,2,1,0:T(8,128)S(1)} %copy-done, ...), custom_call_target="tpu_custom_call" | custom-call | tf_op jit(solution)/shard_map/stage_F/pallas_call | solution.py:253
  38.1 1.3 %collective-permute-start.4 = (f32[4,128,256]{2,1,0:T(8,128)S(1)}, f32[4,128,256]{2,1,0:T(8,128)S(1)}, u32[]{:S(2)}, u32[]{:S(2)}) collective-permute-start(f32[4,128,256]{2,1,0:T(8,128)S(1)} %get-tuple-element.26), channel_id=1, source_target_pairs={{0,16},{8,24},{1,17},{9,25},{2,18},{10,26},{3,19},{11,27},{4,20},{... | collective-permute-start | bytes 1572872 | tf_op jit(solution)/shard_map/ppermute | solution.py:293
  39.4 11.6 %collective-permute-done.4.refs_2_ = f32[4,128,256]{2,1,0:T(8,128)S(1)} collective-permute-done((f32[4,128,256]{2,1,0:T(8,128)S(1)}, f32[4,128,256]{2,1,0:T(8,128)S(1)}, u32[]{:S(2)}, u32[]{:S(2)}) %collective-permute-start.4) | collective-permute-done | bytes 524320 | tf_op jit(solution)/shard_map/ppermute | solution.py:293
  51.0 0.0 copy-done.2
  51.0 0.7 stage_T.1
  51.6 1.3 %collective-permute-start.5 = (f32[4,128,256]{2,1,0:T(8,128)S(1)}, f32[4,128,256]{2,1,0:T(8,128)S(1)}, u32[]{:S(2)}, u32[]{:S(2)}) collective-permute-start(f32[4,128,256]{2,1,0:T(8,128)S(1)} %get-tuple-element.27), channel_id=1, source_target_pairs={{16,0},{24,8},{17,1},{25,9},{18,2},{26,10},{19,3},{27,11},{20,4},{... | collective-permute-start | bytes 1572872 | tf_op jit(solution)/shard_map/ppermute | solution.py:293
  52.9 32.0 %collective-permute-done.5.refs_2_ = f32[4,128,256]{2,1,0:T(8,128)S(1)} collective-permute-done((f32[4,128,256]{2,1,0:T(8,128)S(1)}, f32[4,128,256]{2,1,0:T(8,128)S(1)}, u32[]{:S(2)}, u32[]{:S(2)}) %collective-permute-start.5) | collective-permute-done | bytes 524320 | tf_op jit(solution)/shard_map/ppermute | solution.py:293
  85.0 10.8 %stage_B.1 = (f32[4,128,256]{2,1,0:T(8,128)}, f32[3,2,256,256]{3,2,1,0:T(8,128)}, f32[3,2,256,256]{3,2,1,0:T(8,128)}, f32[3,2,256,128]{3,2,1,0:T(8,128)S(1)}, f32[3,2,256,128]{3,2,1,0:T(8,128)S(1)}) custom-call(s32[12]{0:T(128)S(1)} %concatenate.16.refs_0_, ...), custom_call_target="tpu_custom_call", output_to_operand_aliasing={{1}: (8, {}), {2}: (9, {}), {3}: (10, {}), {4}: (11, {})} | custom-call | tf_op jit(solution)/shard_map/stage_B/pallas_call | solution.py:253
  95.8 0.0 copy-start.6
  95.8 0.0 copy-start.5
  95.8 0.0 copy-start.3
  95.8 0.1 collective-permute-start.7
  95.9 0.5 collective-permute-start.6
  96.4 2.1 %collective-permute-done.7 = f32[3,2,256,128]{3,2,1,0:T(8,128)S(1)} collective-permute-done((f32[3,2,256,128]{3,2,1,0:T(8,128)S(1)}, f32[3,2,256,128]{3,2,1,0:T(8,128)S(1)}, u32[]{:S(2)}, u32[]{:S(2)}) %collective-permute-start.7) | collective-permute-done | bytes 786464 | tf_op jit(solution)/shard_map/ppermute | solution.py:289
  98.5 1.0 add.29
  99.5 0.3 collective-permute-start.8
  99.8 0.0 copy-done.6
  99.8 0.6 dynamic-slice.8
  101.1 0.1 slice_reduce_fusion
  101.2 0.2 dynamic-update-slice.3
  101.5 6.0 %all-reduce = f32[16]{0:T(128)S(1)} all-reduce(f32[16]{0:T(128)S(1)} %dynamic-update-slice.3), channel_id=2, replica_groups=mesh['depth'=4,'lat'=8] {'depth'}, use_global_device_ids=true, to_apply=%add | all-reduce | flops 16 | bytes 128
  107.5 0.1 slice.51
  107.6 1.2 gather_fusion
  108.7 0.0 collective-permute-done.6
  108.7 0.2 add.28
  108.9 13.8 %collective-permute-done.8 = f32[3,2,256,128]{3,2,1,0:T(8,128)} collective-permute-done((f32[3,2,256,128]{3,2,1,0:T(8,128)}, f32[3,2,256,128]{3,2,1,0:T(8,128)}, u32[]{:S(2)}, u32[]{:S(2)}) %collective-permute-start.8) | collective-permute-done | bytes 786464 | tf_op jit(solution)/shard_map/ppermute | solution.py:336
  122.8 1.3 %fusion = f32[3,2,256,256]{3,2,1,0:T(8,128)S(1)} fusion(f32[3,2,256,256]{3,2,1,0:T(8,128)S(1)} %add.28, f32[3,2,256,128]{3,2,1,0:T(8,128)} %collective-permute-done.8), kind=kLoop, calls=%fused_computation.2 | loop fusion | flops 196608 | bytes 2359296 | tf_op jit(solution)/shard_map/scatter-add | solution.py:337
  124.1 0.0 copy-start.4
  124.1 1.1 copy-done.4
  (7 shorter events, 0.1 us)
Async XLA Ops:
  0.6 7.4 %copy-start = (f32[3,2,256,256]{3,2,1,0:T(8,128)S(1)}, f32[3,2,256,256]{3,2,1,0:T(8,128)}, u32[]{:S(2)}) copy-start(f32[3,2,256,256]{3,2,1,0:T(8,128)} %refs_3_.5) | copy-start | bytes 4718596
  0.6 28.6 %copy-start.1 = (bf16[2,2,2,256,256]{4,3,2,1,0:T(8,128)(2,1)S(1)}, bf16[2,2,2,256,256]{4,3,2,1,0:T(8,128)(2,1)}, u32[]{:S(2)}) copy-start(bf16[2,2,2,256,256]{4,3,2,1,0:T(8,128)(2,1)} %constant.47.clone.refs_1_) | copy-start | bytes 3145732
  2.0 22.8 %collective-permute-start.2 = (f32[3,2,256,128]{3,2,1,0:T(8,128)S(1)}, f32[3,2,256,128]{3,2,1,0:T(8,128)S(1)}, u32[]{:S(2)}, u32[]{:S(2)}) collective-permute-start(f32[3,2,256,128]{3,2,1,0:T(8,128)S(1)} %slice.46), channel_id=1, source_target_pairs={{1,0},{2,1},{3,2},{4,3},{5,4},{6,5},{7,6},{0,7},{9,8},{10,9},{11,1... | collective-permute-start | bytes 2359304 | tf_op jit(solution)/shard_map/ppermute | solution.py:295
  8.0 21.1 %collective-permute-start.1 = (f32[3,2,256,256]{3,2,1,0:T(8,128)S(1)}, f32[3,2,256,256]{3,2,1,0:T(8,128)}, u32[]{:S(2)}, u32[]{:S(2)}) collective-permute-start(f32[3,2,256,256]{3,2,1,0:T(8,128)S(1)} %copy-done), channel_id=1, source_target_pairs={{0,8},{8,0},{16,24},{24,16},{1,9},{9,1},{17,25},{25,17},{2,10},{10... | collective-permute-start | bytes 4718600 | tf_op jit(solution)/shard_map/ppermute | solution.py:289
  24.8 4.3 %collective-permute-start.3 = (f32[3,2,256,128]{3,2,1,0:T(8,128)S(1)}, f32[3,2,256,128]{3,2,1,0:T(8,128)}, u32[]{:S(2)}, u32[]{:S(2)}) collective-permute-start(f32[3,2,256,128]{3,2,1,0:T(8,128)S(1)} %collective-permute-done.2.refs_5_), channel_id=1, source_target_pairs={{0,8},{8,0},{16,24},{24,16},{1,9},{9,1},{17,25},{25,17},{2,10},{10... | collective-permute-start | bytes 2359304 | tf_op jit(solution)/shard_map/ppermute | solution.py:289
  24.8 3.5 %collective-permute-start = (s32[1]{0:T(128)}, s32[1]{0:T(128)}, u32[]{:S(2)}, u32[]{:S(2)}) collective-permute-start(s32[1]{0:T(128)} %param.11), channel_id=1, source_target_pairs={{0,8},{8,0},{16,24},{24,16},{1,9},{9,1},{17,25},{25,17},{2,10},{10... | collective-permute-start | bytes 20 | tf_op jit(solution)/shard_map/ppermute | solution.py:289
  29.2 21.7 %copy-start.2 = (f32[8,128,128]{2,1,0:T(8,128)S(1)}, f32[8,128,128]{2,1,0:T(8,128)}, u32[]{:S(2)}) copy-start(f32[8,128,128]{2,1,0:T(8,128)} %refs_7_.1) | copy-start | bytes 1572868
  38.1 12.9 %collective-permute-start.4 = (f32[4,128,256]{2,1,0:T(8,128)S(1)}, f32[4,128,256]{2,1,0:T(8,128)S(1)}, u32[]{:S(2)}, u32[]{:S(2)}) collective-permute-start(f32[4,128,256]{2,1,0:T(8,128)S(1)} %get-tuple-element.26), channel_id=1, source_target_pairs={{0,16},{8,24},{1,17},{9,25},{2,18},{10,26},{3,19},{11,27},{4,20},{... | collective-permute-start | bytes 1572872 | tf_op jit(solution)/shard_map/ppermute | solution.py:293
  51.6 33.3 %collective-permute-start.5 = (f32[4,128,256]{2,1,0:T(8,128)S(1)}, f32[4,128,256]{2,1,0:T(8,128)S(1)}, u32[]{:S(2)}, u32[]{:S(2)}) collective-permute-start(f32[4,128,256]{2,1,0:T(8,128)S(1)} %get-tuple-element.27), channel_id=1, source_target_pairs={{16,0},{24,8},{17,1},{25,9},{18,2},{26,10},{19,3},{27,11},{20,4},{... | collective-permute-start | bytes 1572872 | tf_op jit(solution)/shard_map/ppermute | solution.py:293
  95.8 4.0 %copy-start.6 = (u32[32]{0:T(128)S(1)}, u32[32]{0:T(128)}, u32[]{:S(2)}) copy-start(u32[32]{0:T(128)} %constant.53) | copy-start | bytes 388
  95.8 5.3 %copy-start.5 = (s32[1,8]{1,0:T(1,128)S(1)}, s32[1,8]{1,0:T(1,128)}, u32[]{:S(2)}) copy-start(s32[1,8]{1,0:T(1,128)} %param.14) | copy-start | bytes 100
  95.8 12.9 %copy-start.3 = (f32[3,2,256,256]{3,2,1,0:T(8,128)S(1)}, f32[3,2,256,256]{3,2,1,0:T(8,128)}, u32[]{:S(2)}) copy-start(f32[3,2,256,256]{3,2,1,0:T(8,128)} %get-tuple-element.33) | copy-start | bytes 4718596
  95.8 2.7 %collective-permute-start.7 = (f32[3,2,256,128]{3,2,1,0:T(8,128)S(1)}, f32[3,2,256,128]{3,2,1,0:T(8,128)S(1)}, u32[]{:S(2)}, u32[]{:S(2)}) collective-permute-start(f32[3,2,256,128]{3,2,1,0:T(8,128)S(1)} %get-tuple-element.36), channel_id=1, source_target_pairs={{0,8},{8,0},{16,24},{24,16},{1,9},{9,1},{17,25},{25,17},{2,10},{10... | collective-permute-start | bytes 2359304 | tf_op jit(solution)/shard_map/ppermute | solution.py:289
  95.9 12.8 %collective-permute-start.6 = (f32[3,2,256,256]{3,2,1,0:T(8,128)}, f32[3,2,256,256]{3,2,1,0:T(8,128)S(1)}, u32[]{:S(2)}, u32[]{:S(2)}) collective-permute-start(f32[3,2,256,256]{3,2,1,0:T(8,128)} %get-tuple-element.34), channel_id=1, source_target_pairs={{0,8},{8,0},{16,24},{24,16},{1,9},{9,1},{17,25},{25,17},{2,10},{10... | collective-permute-start | bytes 4718600 | tf_op jit(solution)/shard_map/ppermute | solution.py:289
  99.5 23.3 %collective-permute-start.8 = (f32[3,2,256,128]{3,2,1,0:T(8,128)}, f32[3,2,256,128]{3,2,1,0:T(8,128)}, u32[]{:S(2)}, u32[]{:S(2)}) collective-permute-start(f32[3,2,256,128]{3,2,1,0:T(8,128)} %add.29), channel_id=1, source_target_pairs={{0,1},{1,2},{2,3},{3,4},{4,5},{5,6},{6,7},{7,0},{8,9},{9,10},{10,1... | collective-permute-start | bytes 2359304 | tf_op jit(solution)/shard_map/ppermute | solution.py:336
  124.1 1.1 copy-start.4
where the time goes:
time: 123 us; the launch traced here: 125 us
  waiting for transfers between devices  76.4 us (62%)
  Pallas kernels  20.3 us (17%)
  starting transfers between devices  10 us (8%)
  local copies, waits for them, and re-layouts  7.13 us (6%)
  blocking collectives  6.03 us (5%)
  other arithmetic  3.26 us (3%)
  between operations  2.14 us (2%)
    ppermute x2, waiting for transfers between devices, move(): return lax.ppermute(block, 'depth', route)  43.6 us
    pallas_call x3, Pallas kernels, stage_call(): pl.pallas_call(body, out_shape=outs, in_specs=[scalars] + [anywhere] * (l...  20.3 us
    ppermute x1, waiting for transfers between devices, shards(): lax.ppermute(slices[..., :width], 'lat', [((i + 1) % lat, i) for i in ran...  16.8 us
    ppermute x1, waiting for transfers between devices, shards(): lax.ppermute(over, 'lat', [(i, (i + 1) % lat) for i in range(lat)])  13.8 us
    unnamed x1, blocking collectives  6.03 us
    ppermute x1, starting transfers between devices, shards(): lax.ppermute(slices[..., :width], 'lat', [((i + 1) % lat, i) for i in ran...  6.03 us
    ppermute x2, starting transfers between devices, move(): return lax.ppermute(block, 'depth', route)  2.61 us
  transfers between devices with their start and end apart: 9, of which 5 were waited for; matrix products, arithmetic and copies ran while one was open for 5% of the time, Pallas kernels for 0%

commit v1 on v0

--- a/solution.py
+++ b/solution.py
@@ -70,14 +70,19 @@
     ]
 
 
-def stage_kernel(kind, stage, cfg, *refs):
-    group, slots, width, tile, share = cfg
+def stage_kernel(kind, stage, batch, cfg, *refs):
+    group, slots, width, tile, share, batches = cfg
     blocks = tile // width
-    refs = list(refs)
-    meta, tables_hbm, entering_hbm = refs[:3]
-    mains, rims = refs[3 : 3 + group], refs[3 + group : 3 + 2 * group]
-    refs = refs[3 + 2 * group :]
+    counts, (rows, columns, tables_hbm, entering_hbm), refs = (
+        refs[:group],
+        refs[group : group + 4],
+        list(refs[group + 4 :]),
+    )
+    mains, rims = refs[:group], refs[group : 2 * group]
+    refs = refs[2 * group :]
     if kind == "T":
+        if batch:
+            kept, refs = [refs[1 + i] for i in range(2 * group)], refs[:1] + refs[1 + 2 * group :]
         measured_hbm, out_hbm, loss_ref = refs[0], refs[1], refs[2 + 2 * group]
         grads = refs[2 : 2 + 2 * group]
         refs = refs[3 + 2 * group :]
@@ -85,15 +90,18 @@
         out_hbm, inner_hbm = refs[0], refs[1]
         refs = refs[2:]
     else:
-        inner_hbm = refs[0]
+        inner_hbm, kept = refs[0], refs[1 : 1 + 2 * group]
         out_hbm = refs[1 + 2 * group]
         grads = refs[2 + 2 * group : 2 + 4 * group]
         refs = refs[2 + 4 * group :]
     specimen, store, inner, current, tables, wanted, sems = refs
 
-    @pl.when(meta[0] == stage)
+    segment = lax.axis_index("depth")
+    core = lax.rem(segment, group)
+
+    @pl.when(lax.div(segment, group) == stage)
     def _():
-        core = meta[1]
+        base = (core * batches + batch) * share
         copies = []
 
         def bring(source, target):
@@ -111,18 +119,32 @@
         if kind == "B":
             bring(entering_hbm, current)
             bring(inner_hbm, inner)
+        elif stage == 0:
+            for p in range(share):
+                for c in range(2):
+                    bring(entering_hbm.at[c], inner.at[0, p, :, pl.ds(c * width, width)])
         else:
             bring(entering_hbm, inner.at[0])
         if kind == "T":
-            bring(measured_hbm.at[pl.ds(core * share, share)], wanted)
-        if kind != "F":
+            bring(measured_hbm.at[pl.ds(base, share)], wanted)
+        if kind != "F" and batch:
+            for j in range(group):
+                section = core if j == 0 else 1 - core
+                place = pl.ds(section * slots, slots)
+                for b in range(blocks):
+                    bring(kept[j].at[:, :, :, pl.ds(b * width, width)], store.at[place, :, b])
+                bring(kept[group + j], store.at[place, :, blocks])
+        elif kind != "F":
             for slot in range(group * slots):
                 store[slot] = jnp.zeros(store.shape[1:], jnp.float32)
         for copy in copies:
             copy.wait()
 
-        count = meta[2]
-        total = meta[2] + meta[3] if group == 2 else meta[2]
+        count = counts[0][0]
+        total = count
+        if group == 2:
+            total = counts[0][0] + counts[1][0]
+            count = jnp.where(core == 0, counts[0][0], counts[1][0])
         lane = lax.broadcasted_iota(jnp.int32, (width, width), 1)
 
         def place_of(step):
@@ -130,7 +152,7 @@
             return jnp.where(later, slots + step - count, step)
 
         def corner(p):
-            row, column = meta[4 + p], meta[4 + share + p]
+            row, column = rows[base + p], columns[base + p]
             block = jnp.minimum(column // width, blocks - 1)
             return row, block, column - block * width
 
@@ -221,8 +243,8 @@
             copy.wait()
 
 
-def stage_call(kind, stage, cfg, operands, kept=()):
-    group, slots, width, tile, share = cfg
+def stage_call(kind, stage, batch, cfg, operands, kept=()):
+    group, slots, width, tile, share, batches = cfg
     blocks = tile // width
     f32 = jnp.float32
     field = jax.ShapeDtypeStruct((share, width, 2 * width), f32)
@@ -243,17 +265,17 @@
     for i in range(len(kept)):
         aliases[len(operands) + i] = 1 + i
     operands = list(operands) + list(kept)
-    body = functools.partial(stage_kernel, kind, stage, cfg)
+    body = functools.partial(stage_kernel, kind, stage, batch, cfg)
     if kind == "F" and kept:
         at = len(operands) - 1
 
         def body(*refs):
-            stage_kernel(kind, stage, cfg, *refs[:at], *refs[at + 1 :])
+            stage_kernel(kind, stage, batch, cfg, *refs[:at], *refs[at + 1 :])
 
     return pl.pallas_call(
         body,
         out_shape=outs,
-        in_specs=[scalars] + [anywhere] * (len(operands) - 1),
+        in_specs=[scalars] * (group + 2) + [anywhere] * (len(operands) - group - 2),
         out_specs=out_specs,
         input_output_aliases=aliases,
         scratch_shapes=[
@@ -263,9 +285,12 @@
             pltpu.VMEM((share, width, 2 * width), f32),
             pltpu.VMEM((2, 2, 2, 2 * width, 2 * width), jnp.bfloat16),
             pltpu.VMEM((share, width, width), f32),
-            pltpu.SemaphoreType.DMA((8 + group * (blocks + 1),)),
+            pltpu.SemaphoreType.DMA((4 + 2 * share + 2 * group * (blocks + 1),)),
         ],
         compiler_params=pltpu.CompilerParams(vmem_limit_bytes=48 * 1024 * 1024),
+        cost_estimate=pl.CostEstimate(
+            flops=5_000_000_000, bytes_accessed=10_000_000, transcendentals=0
+        ),
         name="stage_" + kind,
     )(*operands)
 
@@ -278,11 +303,9 @@
     lat = lax.axis_size("lat")
     group = 2 if depth % 2 == 0 and positions % 2 == 0 else 1
     stages = depth // group
-    share = positions // group
-    cfg = (group, slots, width, tile, share)
-    segment = lax.axis_index("depth")
-    core = lax.rem(segment, group)
-    stage = lax.div(segment, group)
+    batches = 2 if positions // group % 2 == 0 else 1
+    share = positions // (group * batches)
+    cfg = (group, slots, width, tile, share, batches)
     swap = [(d, d + 1 - 2 * (d % 2)) for d in range(depth)]
 
     def partner(block):
@@ -295,40 +318,40 @@
     rim = lax.ppermute(slices[..., :width], "lat", [((i + 1) % lat, i) for i in range(lat)])
     if group == 2:
         mains, rims = [slices, partner(slices)], [rim, partner(rim)]
-        other = partner(section_counts)
-        counts = jnp.where(
-            core == 0,
-            jnp.concatenate([section_counts, other]),
-            jnp.concatenate([other, section_counts]),
+        counts = [section_counts, partner(section_counts)]
+    else:
+        mains, rims, counts = [slices], [rim], [section_counts]
+    tables = jnp.asarray(make_tables(width))
+    scalars = (*counts, scan_rows, scan_columns, tables)
+    shared = (*mains, *rims)
+    every = range(batches)
+    fields = [illumination] * batches
+    inner = [()] * batches
+    for s in range(stages - 1):
+        for b in every:
+            field, kept = stage_call("F", s, b, cfg, (*scalars, fields[b], *shared), inner[b])
+            inner[b] = (kept,)
+            fields[b] = move(field, s, s + 1)
+    last = stages - 1
+    pulls, losses, grads = [], [], ()
+    for b in every:
+        pull, *grads, loss = stage_call(
+            "T", last, b, cfg, (*scalars, fields[b], *shared, measured), tuple(grads)
         )
-    else:
-        mains, rims = [slices], [rim]
-        counts = jnp.concatenate([section_counts, jnp.zeros_like(section_counts)])
-    meta = jnp.concatenate(
-        [
-            jnp.stack([stage, core]),
-            counts,
-            lax.dynamic_slice_in_dim(scan_rows, core * share, share, 0),
-            lax.dynamic_slice_in_dim(scan_columns, core * share, share, 0),
-        ]
-    ).astype(jnp.int32)
-    tables = jnp.asarray(make_tables(width))
-    launch = jnp.concatenate([illumination[0], illumination[1]], axis=1)
-    field = jnp.broadcast_to(launch, (share, width, 2 * width))
-    shared = (*mains, *rims)
-    inner = ()
-    for s in range(stages - 1):
-        field, kept = stage_call("F", s, cfg, (meta, tables, field, *shared), inner)
-        inner = (kept,)
-        field = move(field, s, s + 1)
-    last = stages - 1
-    pull, *grads, loss = stage_call("T", last, cfg, (meta, tables, field, *shared, measured))
-    losses = lax.all_gather(loss[:, 0], "depth", axis=0, tiled=True)[last * group * share :]
+        pulls.append(pull)
+        losses.append(loss[:, 0])
+    own = jnp.concatenate(losses)
+    losses = lax.all_gather(own, "depth", axis=0, tiled=True)[last * positions :]
     for s in range(last - 1, -1, -1):
-        pull = move(pull, s + 1, s)
-        pull, *grads = stage_call(
-            "B", s, cfg, (meta, tables, pull, *shared, inner[0]), tuple(grads)
-        )
+        for b in every:
+            pulls[b], *grads = stage_call(
+                "B",
+                s,
+                b,
+                cfg,
+                (*scalars, move(pulls[b], s + 1, s), *shared, *inner[b]),
+                tuple(grads),
+            )
     main, over = grads[0], grads[group]
     if group == 2:
         over = over + partner(grads[group + 1])

time: 123 us -> 121 us (0.984)
  waiting for transfers between devices: 76.4 us -> 61.3 us
  Pallas kernels: 20.3 us -> 31 us
  starting transfers between devices: 10 us -> 12.8 us
    ppermute x2 -> x4, waiting for transfers between devices: 43.6 us -> 27.5 us  [move(): return lax.ppermute(block, 'depth', route)]
    pallas_call x3 -> x6, Pallas kernels: 20.3 us -> 31 us  [stage_call(): pl.pallas_call(body, out_shape=outs, in_specs=[scalars] * (group + 2) + [...]
    ppermute x2 -> x4, starting transfers between devices: 2.61 us -> 5.33 us  [move(): return lax.ppermute(block, 'depth', route)]
    unnamed x17 -> x24, local copies, waits for them, and re-layouts: 2 us -> 3.89 us
    dynamic_slice x2 -> x0, local copies, waits for them, and re-layouts: 1.46 us -> none  [the longest x1 0.73 us: shards(): lax.dynamic_slice_in_dim(scan_rows, core * share, share, 0)]
  transfers between devices with their start and end apart: 9 -> 11, of which waited for: 5 -> 8; matrix products, arithmetic and copies ran while one was open for 5% -> 3% of each run, Pallas kernels for 0% -> 13%
where the time goes in v1:
time: 121 us; the launch traced here: 123 us
  waiting for transfers between devices  61.3 us (51%)
  Pallas kernels  31 us (26%)
  starting transfers between devices  12.8 us (11%)
  local copies, waits for them, and re-layouts  6.64 us (5%)
  blocking collectives  6.03 us (5%)
  other arithmetic  2.7 us (2%)
  between operations  2.17 us (2%)
    pallas_call x6, Pallas kernels, stage_call(): pl.pallas_call(body, out_shape=outs, in_specs=[scalars] * (group + 2) + [...  31 us
    ppermute x4, waiting for transfers between devices, move(): return lax.ppermute(block, 'depth', route)  27.5 us
    ppermute x1, waiting for transfers between devices, shards(): lax.ppermute(slices[..., :width], 'lat', [((i + 1) % lat, i) for i in ran...  16.8 us
    ppermute x1, waiting for transfers between devices, shards(): lax.ppermute(over, 'lat', [(i, (i + 1) % lat) for i in range(lat)])  13.8 us
    unnamed x1, blocking collectives  6.03 us
    ppermute x1, starting transfers between devices, shards(): lax.ppermute(slices[..., :width], 'lat', [((i + 1) % lat, i) for i in ran...  6.03 us
    ppermute x4, starting transfers between devices, move(): return lax.ppermute(block, 'depth', route)  5.33 us
    unnamed x24, local copies, waits for them, and re-layouts  3.89 us
  transfers between devices with their start and end apart: 11, of which 8 were waited for; matrix products, arithmetic and copies ran while one was open for 3% of the time, Pallas kernels for 13%

profile of v1, /device:TPU:0, one launch (start us, length us, event | category | flops | bytes accessed | tf_op | source)
XLA Modules:
  0.0 122.6 jit_solution(4000697295227651797)
XLA Ops:
  0.6 0.0 copy-start
  0.7 1.3 %slice.41 = f32[3,2,256,128]{3,2,1,0:T(8,128)S(1)} slice(f32[3,2,256,256]{3,2,1,0:T(8,128)} %refs_6_.11), slice={[0:3], [0:2], [0:256], [0:128]} | slice | bytes 1572864 | tf_op jit(solution)/shard_map/slice | solution.py:318
  2.0 6.0 %collective-permute-start.2 = (f32[3,2,256,128]{3,2,1,0:T(8,128)S(1)}, f32[3,2,256,128]{3,2,1,0:T(8,128)S(1)}, u32[]{:S(2)}, u32[]{:S(2)}) collective-permute-start(f32[3,2,256,128]{3,2,1,0:T(8,128)S(1)} %slice.41), channel_id=1, source_target_pairs={{1,0},{2,1},{3,2},{4,3},{5,4},{6,5},{7,6},{0,7},{9,8},{10,9},{11,1... | collective-permute-start | bytes 2359304 | tf_op jit(solution)/shard_map/ppermute | solution.py:318
  8.0 0.0 collective-permute-start.1
  8.0 16.8 %collective-permute-done.2.refs_8_ = f32[3,2,256,128]{3,2,1,0:T(8,128)S(1)} collective-permute-done((f32[3,2,256,128]{3,2,1,0:T(8,128)S(1)}, f32[3,2,256,128]{3,2,1,0:T(8,128)S(1)}, u32[]{:S(2)}, u32[]{:S(2)}) %collective-permute-start.2) | collective-permute-done | bytes 786464 | tf_op jit(solution)/shard_map/ppermute | solution.py:318
  24.8 0.0 collective-permute-start.3
  24.8 0.5 collective-permute-start
  26.0 0.9 collective-permute-done.refs_1_
  26.8 0.2 collective-permute-done.3.refs_9_
  27.1 0.0 collective-permute-done.1.refs_7_
  27.1 0.0 copy-start.3
  27.1 0.9 copy-done.3
  28.0 1.2 copy-done.6
  29.2 5.3 %stage_F.3 = (f32[2,128,256]{2,1,0:T(8,128)S(1)}, f32[7,2,128,256]{3,2,1,0:T(8,128)}) custom-call(s32[1]{0:T(128)S(6)} %copy.36.refs_0_, s32[1]{0:T(128)} %collective-permute-done.refs_1_, s32[8]{0:T(128)S(1)} %copy-done.4, s32[8]{0:T(128)S(1)} %copy-done.5, bf16[2,2,2,256,256]{4,3,2,1,0:T(8,128)(2,1)S(1)} %copy-done.6, f32[2,128,128]{2,1,0:T(8,128)S(1)} %copy-done.3, ...), custom_call_target="tpu_custom_call" | custom-call | flops 5000000000 | bytes 10000000 | tf_op jit(solution)/shard_map/stage_F/pallas_call | solution.py:275
  34.6 0.0 copy-start.2
  34.6 1.4 %collective-permute-start.5 = (f32[2,128,256]{2,1,0:T(8,128)S(1)}, f32[2,128,256]{2,1,0:T(8,128)S(1)}, u32[]{:S(2)}, u32[]{:S(2)}) collective-permute-start(f32[2,128,256]{2,1,0:T(8,128)S(1)} %get-tuple-element.39), channel_id=1, source_target_pairs={{0,16},{8,24},{1,17},{9,25},{2,18},{10,26},{3,19},{11,27},{4,20},{... | collective-permute-start | bytes 786440 | tf_op jit(solution)/shard_map/ppermute | solution.py:316
  36.0 5.4 %stage_F.2 = (f32[2,128,256]{2,1,0:T(8,128)S(1)}, f32[7,2,128,256]{3,2,1,0:T(8,128)}) custom-call(s32[1]{0:T(128)S(6)} %copy.36.refs_0_, s32[1]{0:T(128)} %collective-permute-done.refs_1_, s32[8]{0:T(128)S(1)} %copy-done.4, s32[8]{0:T(128)S(1)} %copy-done.5, bf16[2,2,2,256,256]{4,3,2,1,0:T(8,128)(2,1)S(1)} %copy-done.6, f32[2,128,128]{2,1,0:T(8,128)S(1)} %copy-done.3, ...), custom_call_target="tpu_custom_call" | custom-call | flops 5000000000 | bytes 10000000 | tf_op jit(solution)/shard_map/stage_F/pallas_call | solution.py:275
  41.4 1.3 %collective-permute-start.4 = (f32[2,128,256]{2,1,0:T(8,128)S(1)}, f32[2,128,256]{2,1,0:T(8,128)S(1)}, u32[]{:S(2)}, u32[]{:S(2)}) collective-permute-start(f32[2,128,256]{2,1,0:T(8,128)S(1)} %get-tuple-element.38), channel_id=1, source_target_pairs={{0,16},{8,24},{1,17},{9,25},{2,18},{10,26},{3,19},{11,27},{4,20},{... | collective-permute-start | bytes 786440 | tf_op jit(solution)/shard_map/ppermute | solution.py:316
  42.7 0.0 collective-permute-done.5.refs_5_
  42.8 1.4 %stage_T.2 = (f32[2,128,256]{2,1,0:T(8,128)S(1)}, f32[3,2,256,256]{3,2,1,0:T(8,128)}, f32[3,2,256,256]{3,2,1,0:T(8,128)}, f32[3,2,256,128]{3,2,1,0:T(8,128)S(1)}...) custom-call(s32[1]{0:T(128)S(6)} %copy.36.refs_0_, s32[1]{0:T(128)} %collective-permute-done.refs_1_, ...), custom_call_target="tpu_custom_call" | custom-call | flops 5000000000 | bytes 10000000 | tf_op jit(solution)/shard_map/stage_T/pallas_call | solution.py:275
  44.1 1.3 %collective-permute-start.7 = (f32[2,128,256]{2,1,0:T(8,128)S(1)}, f32[2,128,256]{2,1,0:T(8,128)S(1)}, u32[]{:S(2)}, u32[]{:S(2)}) collective-permute-start(f32[2,128,256]{2,1,0:T(8,128)S(1)} %get-tuple-element.46), channel_id=1, source_target_pairs={{16,0},{24,8},{17,1},{25,9},{18,2},{26,10},{19,3},{27,11},{20,4},{... | collective-permute-start | bytes 786440 | tf_op jit(solution)/shard_map/ppermute | solution.py:316
  45.4 3.4 %collective-permute-done.4.refs_5_ = f32[2,128,256]{2,1,0:T(8,128)S(1)} collective-permute-done((f32[2,128,256]{2,1,0:T(8,128)S(1)}, f32[2,128,256]{2,1,0:T(8,128)S(1)}, u32[]{:S(2)}, u32[]{:S(2)}) %collective-permute-start.4) | collective-permute-done | bytes 262176 | tf_op jit(solution)/shard_map/ppermute | solution.py:316
  48.9 1.4 %stage_T.3 = (f32[2,128,256]{2,1,0:T(8,128)S(1)}, f32[3,2,256,256]{3,2,1,0:T(8,128)}, f32[3,2,256,256]{3,2,1,0:T(8,128)}, f32[3,2,256,128]{3,2,1,0:T(8,128)S(1)}...) custom-call(s32[1]{0:T(128)S(6)} %copy.36.refs_0_, ...), custom_call_target="tpu_custom_call", output_to_operand_aliasing={{1}: (11, {}), {2}: (12, {}), {3}: (13, {}), {4}: (14, {})} | custom-call | flops 5000000000 | bytes 10000000 | tf_op jit(solution)/shard_map/stage_T/pallas_call | solution.py:275
  50.2 1.3 %collective-permute-start.6 = (f32[2,128,256]{2,1,0:T(8,128)S(1)}, f32[2,128,256]{2,1,0:T(8,128)S(1)}, u32[]{:S(2)}, u32[]{:S(2)}) collective-permute-start(f32[2,128,256]{2,1,0:T(8,128)S(1)} %get-tuple-element.44), channel_id=1, source_target_pairs={{16,0},{24,8},{17,1},{25,9},{18,2},{26,10},{19,3},{27,11},{20,4},{... | collective-permute-start | bytes 786440 | tf_op jit(solution)/shard_map/ppermute | solution.py:316
  51.5 15.2 %collective-permute-done.7.refs_5_ = f32[2,128,256]{2,1,0:T(8,128)S(1)} collective-permute-done((f32[2,128,256]{2,1,0:T(8,128)S(1)}, f32[2,128,256]{2,1,0:T(8,128)S(1)}, u32[]{:S(2)}, u32[]{:S(2)}) %collective-permute-start.7) | collective-permute-done | bytes 262176 | tf_op jit(solution)/shard_map/ppermute | solution.py:316
  66.7 8.3 %stage_B.2 = (f32[2,128,256]{2,1,0:T(8,128)}, f32[3,2,256,256]{3,2,1,0:T(8,128)}, f32[3,2,256,256]{3,2,1,0:T(8,128)}, f32[3,2,256,128]{3,2,1,0:T(8,128)S(1)}, f32[3,2,256,128]{3,2,1,0:T(8,128)S(1)}) custom-call(s32[1]{0:T(128)S(6)} %copy.36.refs_0_, ...), custom_call_target="tpu_custom_call", output_to_operand_aliasing={{1}: (11, {}), {2}: (12, {}), {3}: (13, {}), {4}: (14, {})} | custom-call | flops 5000000000 | bytes 10000000 | tf_op jit(solution)/shard_map/stage_B/pallas_call | solution.py:275
  75.0 8.9 %collective-permute-done.6.refs_5_ = f32[2,128,256]{2,1,0:T(8,128)S(1)} collective-permute-done((f32[2,128,256]{2,1,0:T(8,128)S(1)}, f32[2,128,256]{2,1,0:T(8,128)S(1)}, u32[]{:S(2)}, u32[]{:S(2)}) %collective-permute-start.6) | collective-permute-done | bytes 262176 | tf_op jit(solution)/shard_map/ppermute | solution.py:316
  83.9 9.2 %stage_B.3 = (f32[2,128,256]{2,1,0:T(8,128)}, f32[3,2,256,256]{3,2,1,0:T(8,128)}, f32[3,2,256,256]{3,2,1,0:T(8,128)}, f32[3,2,256,128]{3,2,1,0:T(8,128)S(1)}, f32[3,2,256,128]{3,2,1,0:T(8,128)S(1)}) custom-call(s32[1]{0:T(128)S(6)} %copy.36.refs_0_, ...), custom_call_target="tpu_custom_call", output_to_operand_aliasing={{1}: (11, {}), {2}: (12, {}), {3}: (13, {}), {4}: (14, {})} | custom-call | flops 5000000000 | bytes 10000000 | tf_op jit(solution)/shard_map/stage_B/pallas_call | solution.py:275
  93.1 0.0 copy-start.10
  93.1 0.0 copy-start.9
  93.2 0.1 collective-permute-start.9
  93.2 0.5 collective-permute-start.8
  93.7 2.1 %collective-permute-done.9 = f32[3,2,256,128]{3,2,1,0:T(8,128)S(1)} collective-permute-done((f32[3,2,256,128]{3,2,1,0:T(8,128)S(1)}, f32[3,2,256,128]{3,2,1,0:T(8,128)S(1)}, u32[]{:S(2)}, u32[]{:S(2)}) %collective-permute-start.9) | collective-permute-done | bytes 786464 | tf_op jit(solution)/shard_map/ppermute | solution.py:312
  95.8 1.0 add.24
  96.8 0.3 collective-permute-start.10
  97.2 0.6 dynamic-slice.8
  98.4 0.1 slice_reduce_fusion
  98.5 0.1 slice_reduce_fusion.1
  98.7 0.2 maximum_dynamic-update-slice_fusion
  98.8 6.0 %all-reduce = f32[16]{0:T(128)S(1)} all-reduce(f32[16]{0:T(128)S(1)} %maximum_dynamic-update-slice_fusion), channel_id=1, replica_groups=mesh['depth'=4,'lat'=8] {'depth'}, use_global_device_ids=true, to_apply=%add | all-reduce | flops 16 | bytes 128
  104.9 0.1 slice.45
  104.9 1.2 gather_fusion
  106.1 0.0 collective-permute-done.8
  106.1 0.2 add.23
  106.3 13.8 %collective-permute-done.10 = f32[3,2,256,128]{3,2,1,0:T(8,128)} collective-permute-done((f32[3,2,256,128]{3,2,1,0:T(8,128)}, f32[3,2,256,128]{3,2,1,0:T(8,128)}, u32[]{:S(2)}, u32[]{:S(2)}) %collective-permute-start.10) | collective-permute-done | bytes 786464 | tf_op jit(solution)/shard_map/ppermute | solution.py:359
  120.1 1.3 %fusion = f32[3,2,256,256]{3,2,1,0:T(8,128)S(1)} fusion(f32[3,2,256,256]{3,2,1,0:T(8,128)S(1)} %add.23, f32[3,2,256,128]{3,2,1,0:T(8,128)} %collective-permute-done.10), kind=kLoop, calls=%fused_computation.2 | loop fusion | flops 196608 | bytes 2359296 | tf_op jit(solution)/shard_map/scatter-add | solution.py:360
  121.4 0.0 copy-start.7
  121.5 1.1 copy-done.7
  (16 shorter events, 0.0 us)
Async XLA Ops:
  0.6 7.4 %copy-start = (f32[3,2,256,256]{3,2,1,0:T(8,128)S(1)}, f32[3,2,256,256]{3,2,1,0:T(8,128)}, u32[]{:S(2)}) copy-start(f32[3,2,256,256]{3,2,1,0:T(8,128)} %refs_6_.11) | copy-start | bytes 4718596
  0.6 26.4 %copy-start.4 = (s32[8]{0:T(128)S(1)}, s32[8]{0:T(128)}, u32[]{:S(2)}) copy-start(s32[8]{0:T(128)} %refs_2_.11) | copy-start | bytes 100
  0.7 26.4 %copy-start.5 = (s32[8]{0:T(128)S(1)}, s32[8]{0:T(128)}, u32[]{:S(2)}) copy-start(s32[8]{0:T(128)} %refs_3_.11) | copy-start | bytes 100
  2.0 22.8 %collective-permute-start.2 = (f32[3,2,256,128]{3,2,1,0:T(8,128)S(1)}, f32[3,2,256,128]{3,2,1,0:T(8,128)S(1)}, u32[]{:S(2)}, u32[]{:S(2)}) collective-permute-start(f32[3,2,256,128]{3,2,1,0:T(8,128)S(1)} %slice.41), channel_id=1, source_target_pairs={{1,0},{2,1},{3,2},{4,3},{5,4},{6,5},{7,6},{0,7},{9,8},{10,9},{11,1... | collective-permute-start | bytes 2359304 | tf_op jit(solution)/shard_map/ppermute | solution.py:318
  8.0 19.1 %collective-permute-start.1 = (f32[3,2,256,256]{3,2,1,0:T(8,128)S(1)}, f32[3,2,256,256]{3,2,1,0:T(8,128)S(1)}, u32[]{:S(2)}, u32[]{:S(2)}) collective-permute-start(f32[3,2,256,256]{3,2,1,0:T(8,128)S(1)} %copy-done), channel_id=1, source_target_pairs={{0,8},{8,0},{16,24},{24,16},{1,9},{9,1},{17,25},{25,17},{2,10},{10... | collective-permute-start | bytes 4718600 | tf_op jit(solution)/shard_map/ppermute | solution.py:312
  24.8 2.3 %collective-permute-start.3 = (f32[3,2,256,128]{3,2,1,0:T(8,128)S(1)}, f32[3,2,256,128]{3,2,1,0:T(8,128)S(1)}, u32[]{:S(2)}, u32[]{:S(2)}) collective-permute-start(f32[3,2,256,128]{3,2,1,0:T(8,128)S(1)} %collective-permute-done.2.refs_8_), channel_id=1, source_target_pairs={{0,8},{8,0},{16,24},{24,16},{1,9},{9,1},{17,25},{25,17},{2,10},{10... | collective-permute-start | bytes 2359304 | tf_op jit(solution)/shard_map/ppermute | solution.py:312
  24.8 2.0 %collective-permute-start = (s32[1]{0:T(128)}, s32[1]{0:T(128)}, u32[]{:S(2)}, u32[]{:S(2)}) collective-permute-start(s32[1]{0:T(128)} %param.11), channel_id=1, source_target_pairs={{0,8},{8,0},{16,24},{24,16},{1,9},{9,1},{17,25},{25,17},{2,10},{10... | collective-permute-start | bytes 20 | tf_op jit(solution)/shard_map/ppermute | solution.py:312
  27.1 0.9 copy-start.3
  28.0 1.2 copy-start.6
  29.2 6.8 %copy-start.1 = (f32[3,2,256,256]{3,2,1,0:T(8,128)}, f32[3,2,256,256]{3,2,1,0:T(8,128)S(1)}, u32[]{:S(2)}) copy-start(f32[3,2,256,256]{3,2,1,0:T(8,128)S(1)} %collective-permute-done.1.refs_7_) | copy-start | bytes 4718596
  34.6 8.2 %copy-start.2 = (f32[8,128,128]{2,1,0:T(8,128)S(1)}, f32[8,128,128]{2,1,0:T(8,128)}, u32[]{:S(2)}) copy-start(f32[8,128,128]{2,1,0:T(8,128)} %refs_10_.3) | copy-start | bytes 1572868
  34.6 8.2 %collective-permute-start.5 = (f32[2,128,256]{2,1,0:T(8,128)S(1)}, f32[2,128,256]{2,1,0:T(8,128)S(1)}, u32[]{:S(2)}, u32[]{:S(2)}) collective-permute-start(f32[2,128,256]{2,1,0:T(8,128)S(1)} %get-tuple-element.39), channel_id=1, source_target_pairs={{0,16},{8,24},{1,17},{9,25},{2,18},{10,26},{3,19},{11,27},{4,20},{... | collective-permute-start | bytes 786440 | tf_op jit(solution)/shard_map/ppermute | solution.py:316
  41.4 7.4 %collective-permute-start.4 = (f32[2,128,256]{2,1,0:T(8,128)S(1)}, f32[2,128,256]{2,1,0:T(8,128)S(1)}, u32[]{:S(2)}, u32[]{:S(2)}) collective-permute-start(f32[2,128,256]{2,1,0:T(8,128)S(1)} %get-tuple-element.38), channel_id=1, source_target_pairs={{0,16},{8,24},{1,17},{9,25},{2,18},{10,26},{3,19},{11,27},{4,20},{... | collective-permute-start | bytes 786440 | tf_op jit(solution)/shard_map/ppermute | solution.py:316
  44.1 22.6 %collective-permute-start.7 = (f32[2,128,256]{2,1,0:T(8,128)S(1)}, f32[2,128,256]{2,1,0:T(8,128)S(1)}, u32[]{:S(2)}, u32[]{:S(2)}) collective-permute-start(f32[2,128,256]{2,1,0:T(8,128)S(1)} %get-tuple-element.46), channel_id=1, source_target_pairs={{16,0},{24,8},{17,1},{25,9},{18,2},{26,10},{19,3},{27,11},{20,4},{... | collective-permute-start | bytes 786440 | tf_op jit(solution)/shard_map/ppermute | solution.py:316
  50.2 33.6 %collective-permute-start.6 = (f32[2,128,256]{2,1,0:T(8,128)S(1)}, f32[2,128,256]{2,1,0:T(8,128)S(1)}, u32[]{:S(2)}, u32[]{:S(2)}) collective-permute-start(f32[2,128,256]{2,1,0:T(8,128)S(1)} %get-tuple-element.44), channel_id=1, source_target_pairs={{16,0},{24,8},{17,1},{25,9},{18,2},{26,10},{19,3},{27,11},{20,4},{... | collective-permute-start | bytes 786440 | tf_op jit(solution)/shard_map/ppermute | solution.py:316
  93.1 4.0 %copy-start.10 = (u32[32]{0:T(128)S(1)}, u32[32]{0:T(128)}, u32[]{:S(2)}) copy-start(u32[32]{0:T(128)} %constant.38) | copy-start | bytes 388
  93.1 5.3 %copy-start.9 = (s32[1,8]{1,0:T(1,128)S(1)}, s32[1,8]{1,0:T(1,128)}, u32[]{:S(2)}) copy-start(s32[1,8]{1,0:T(1,128)} %param.14) | copy-start | bytes 100
  93.1 13.0 %copy-start.8 = (f32[3,2,256,256]{3,2,1,0:T(8,128)S(1)}, f32[3,2,256,256]{3,2,1,0:T(8,128)}, u32[]{:S(2)}) copy-start(f32[3,2,256,256]{3,2,1,0:T(8,128)} %get-tuple-element.56) | copy-start | bytes 4718596
  93.2 2.7 %collective-permute-start.9 = (f32[3,2,256,128]{3,2,1,0:T(8,128)S(1)}, f32[3,2,256,128]{3,2,1,0:T(8,128)S(1)}, u32[]{:S(2)}, u32[]{:S(2)}) collective-permute-start(f32[3,2,256,128]{3,2,1,0:T(8,128)S(1)} %get-tuple-element.59), channel_id=1, source_target_pairs={{0,8},{8,0},{16,24},{24,16},{1,9},{9,1},{17,25},{25,17},{2,10},{10... | collective-permute-start | bytes 2359304 | tf_op jit(solution)/shard_map/ppermute | solution.py:312
  93.2 12.9 %collective-permute-start.8 = (f32[3,2,256,256]{3,2,1,0:T(8,128)}, f32[3,2,256,256]{3,2,1,0:T(8,128)S(1)}, u32[]{:S(2)}, u32[]{:S(2)}) collective-permute-start(f32[3,2,256,256]{3,2,1,0:T(8,128)} %get-tuple-element.57), channel_id=1, source_target_pairs={{0,8},{8,0},{16,24},{24,16},{1,9},{9,1},{17,25},{25,17},{2,10},{10... | collective-permute-start | bytes 4718600 | tf_op jit(solution)/shard_map/ppermute | solution.py:312
  96.8 23.3 %collective-permute-start.10 = (f32[3,2,256,128]{3,2,1,0:T(8,128)}, f32[3,2,256,128]{3,2,1,0:T(8,128)}, u32[]{:S(2)}, u32[]{:S(2)}) collective-permute-start(f32[3,2,256,128]{3,2,1,0:T(8,128)} %add.24), channel_id=1, source_target_pairs={{0,1},{1,2},{2,3},{3,4},{4,5},{5,6},{6,7},{7,0},{8,9},{9,10},{10,1... | collective-permute-start | bytes 2359304 | tf_op jit(solution)/shard_map/ppermute | solution.py:359
  121.4 1.1 copy-start.7
